TPU v7x, 512 devices: a whole 4x8x8 slice. The times are simulated.
512 devices in a mesh: prefix: 16 (over z_lo, y), ctx: 4 (over z_hi), kvh: 8 (over x, core).
Axes of the slice: x: 4, y: 8, z: 8 (z_hi: 4, z_lo: 2; z = z_hi * 2 + z_lo), core: 2. Of those that a mesh axis runs over, the one named last changes fastest.
Arguments:
- queries: bfloat16 [1024, 8192], P(('prefix', 'ctx'), 'kvh'), may hold values from -6.5 to 6.5
- prefix_ids: int32 [1024, 1], P(('prefix', 'ctx')), may hold values from 0 to 15; in each aligned block of 16 rows (0 to 15, 16 to 31, ...) at most 2 rows name the same one
- keys: bfloat16 [16, 16384, 1024], P('prefix', 'ctx', 'kvh'), may hold values from -6 to 6
- values: bfloat16 [16, 16384, 1024], P('prefix', 'ctx', 'kvh'), may hold values from -6 to 6
Outputs:
- attended: bfloat16 [1024, 8192], P(('prefix', 'ctx'), 'kvh')
Inputs may be any that keep to these rules, and one draw needn't show every extreme that they name: `prefix_ids`: in each aligned block of 16 rows (one request device's requests) no prefix is named by more than 2 rows, a bound that some block reaches.
All inputs are finite; a program needn't handle non-finite values.
Results may differ from a plain program's by a relative error of at most 0.0048.
Values may be sent and summed in bfloat16 or wider, within the bound.
A program may use at most 64 MiB of HBM per device.

v0:
```python
import jax
import jax.numpy as jnp
from jax import lax
from jax.sharding import PartitionSpec as P

DH = 128
SEND_CAP = 2
GROUP = 8


def rank_within(pref_ids):
    count = pref_ids.shape[-1]
    same_pref = pref_ids[..., :, None] == pref_ids[..., None, :]
    earlier = jnp.arange(count)[:, None] > jnp.arange(count)[None, :]
    return jnp.sum(same_pref & earlier, axis=-1)


def place_rows(query_rows, pref_ids, n_pre):
    target = pref_ids * SEND_CAP + rank_within(pref_ids)
    one_hot = (jnp.arange(n_pre * SEND_CAP)[:, None] == target[None, :]).astype(jnp.bfloat16)
    placed = jnp.dot(one_hot, query_rows, preferred_element_type=jnp.float32).astype(jnp.bfloat16)
    return placed.reshape(n_pre, SEND_CAP, query_rows.shape[1])


def body(queries, prefix_ids, keys, values):
    n_pre = lax.axis_size("prefix")
    n_ctx = lax.axis_size("ctx")
    own_ids = prefix_ids[:, 0]
    features = queries.shape[1]
    outgoing = place_rows(queries, own_ids, n_pre)
    arrived = lax.all_to_all(outgoing, "prefix", split_axis=0, concat_axis=0, tiled=True)
    group_rows = lax.all_gather(arrived[None], "ctx", axis=0, tiled=True)
    flat_slots = group_rows.reshape(-1, features)
    n_slots = flat_slots.shape[0]
    kv_heads = keys.shape[2] // DH
    queried = flat_slots.reshape(n_slots, kv_heads, GROUP, DH)
    ctx_len = keys.shape[1]
    block_len = max(ctx_len // 8, min(ctx_len, 128))
    n_blocks = ctx_len // block_len
    key_blocks = keys[0].reshape(n_blocks, block_len, kv_heads, DH)
    value_blocks = values[0].reshape(n_blocks, block_len, kv_heads, DH)
    inv_root = DH ** (-0.5)

    def block_scores(key_block):
        return (
            jnp.einsum("sked,tkd->kset", queried, key_block, preferred_element_type=jnp.float32)
            * inv_root
        )

    def max_step(running, key_block):
        return (jnp.maximum(running, jnp.max(block_scores(key_block), axis=-1)), None)

    start_max = jnp.full((kv_heads, n_slots, GROUP), -jnp.inf, jnp.float32)
    local_max, _ = lax.scan(max_step, start_max, key_blocks)
    row_max = lax.pmax(local_max, "ctx")

    def sum_step(running, blocks):
        numer, denom = running
        expo = jnp.exp(block_scores(blocks[0]) - row_max[..., None])
        denom = denom + jnp.sum(expo, axis=-1)
        numer = numer + jnp.einsum(
            "kset,tkd->sked",
            expo.astype(jnp.bfloat16),
            blocks[1],
            preferred_element_type=jnp.float32,
        )
        return ((numer, denom), None)

    start_sums = (
        jnp.zeros((n_slots, kv_heads, GROUP, DH), jnp.float32),
        jnp.zeros((kv_heads, n_slots, GROUP), jnp.float32),
    )
    (numer, denom), _ = lax.scan(sum_step, start_sums, (key_blocks, value_blocks))
    share = n_slots // n_ctx
    numer_split = numer.reshape(n_ctx, share, kv_heads, GROUP, DH)
    denom_split = jnp.transpose(denom, (1, 0, 2)).reshape(n_ctx, share, kv_heads, GROUP)
    totals = lax.psum((numer_split, denom_split), "ctx")
    position = lax.axis_index("ctx")
    mine_numer = lax.dynamic_index_in_dim(totals[0], position, 0, keepdims=False)
    mine_denom = lax.dynamic_index_in_dim(totals[1], position, 0, keepdims=False)
    answer = (
        (mine_numer / mine_denom[..., None]).astype(jnp.bfloat16).reshape(n_pre, SEND_CAP, features)
    )
    returned = lax.all_to_all(answer, "prefix", split_axis=0, concat_axis=0, tiled=True)
    target = own_ids * SEND_CAP + rank_within(own_ids)
    picker = (target[:, None] == jnp.arange(n_pre * SEND_CAP)[None, :]).astype(jnp.bfloat16)
    picked = jnp.dot(
        picker, returned.reshape(n_pre * SEND_CAP, features), preferred_element_type=jnp.float32
    )
    return picked.astype(jnp.bfloat16)


def solution(mesh):
    in_specs = (
        P(("prefix", "ctx"), "kvh"),
        P(("prefix", "ctx"), None),
        P("prefix", "ctx", "kvh"),
        P("prefix", "ctx", "kvh"),
    )
    out_specs = P(("prefix", "ctx"), "kvh")
    return jax.shard_map(body, mesh=mesh, in_specs=in_specs, out_specs=out_specs, check_vma=False)
```

profile of v0, /device:TPU:2, one launch (start us, length us, event | category | flops | bytes accessed | tf_op | source)
XLA Modules:
  0.0 173.4 jit_solution(17465695116124553294)
XLA Ops:
  6.5 0.9 convert_reduce_fusion
  7.4 0.7 multiply_add_fusion
  8.1 0.1 convolution_convert_fusion
  8.3 0.7 reshape.63
  8.9 9.0 %all-to-all-start = ((bf16[16,2,1024]{2,1,0:T(2,128)(2,1)}), bf16[16,2,1024]{2,1,0:T(2,128)(2,1)S(1)}, u32[]{:S(2)}, u32[]{:S(2)}) async-start(bf16[16,2,1024]{2,1,0:T(2,128)(2,1)} %reshape.63), calls=%async_computation | async-start | bytes 131072 | tf_op jit(solution)/shard_map/all_to_all | solution.py:31
  18.0 8.4 %all-to-all-done = bf16[16,2,1024]{2,1,0:T(2,128)(2,1)S(1)} async-done(((bf16[16,2,1024]{2,1,0:T(2,128)(2,1)}), bf16[16,2,1024]{2,1,0:T(2,128)(2,1)S(1)}, u32[]{:S(2)}, u32[]{:S(2)}) %all-to-all-start) | async-done | bytes 65568 | tf_op jit(solution)/shard_map/all_to_all | solution.py:31
  26.5 19.5 %all-gather = bf16[64,2,1024]{2,1,0:T(2,128)(2,1)S(1)} all-gather(bf16[16,2,1024]{2,1,0:T(2,128)(2,1)S(1)} %all-to-all-done), channel_id=2, replica_groups=mesh['prefix'=16,'ctx'=4,'kvh'=8] {'ctx'}, dimensions={0}, use_global_device_ids=true | all-gather | bytes 327680 | tf_op jit(solution)/shard_map/all_gather | solution.py:32
  46.0 0.2 reshape_reshape.3
  46.2 11.1 %while.24 = (s32[]{:T(128)}, f32[1,128,8]{1,2,0:T(8,128)S(1)}, bf16[8,512,1,128]{3,1,2,0:T(8,128)(2,1)}, bf16[128,1,8,128]{3,0,2,1:T(8,128)(2,1)S(1)}, s32[]{:T(128)}, /*index=5*/s32[]{:T(128)}) while((s32[]{:T(128)}, f32[1,128,8]{1,2,0:T(8,128)S(1)}, bf16[8,512,1,128]{3,1,2,0:T(8,128)(2,1)}, ...), condition=%wide.region_3.4_spmd.clone, body=%wide.region_1.3_spmd.clone.sunk | while | flops 135267328 | bytes 410191 | solution.py:54
  46.2 1.4 multiply_reduce_fusion.2
  47.6 1.4 multiply_reduce_fusion.2
  49.0 1.3 multiply_reduce_fusion.2
  50.4 1.3 multiply_reduce_fusion.2
  51.8 1.4 multiply_reduce_fusion.2
  53.2 1.4 multiply_reduce_fusion.2
  54.6 1.4 multiply_reduce_fusion.2
  56.0 1.4 multiply_reduce_fusion.2
  57.3 11.7 %pmax.7 = f32[1,128,8]{1,2,0:T(8,128)S(1)} all-reduce(f32[1,128,8]{1,2,0:T(8,128)S(1)} %get-tuple-element.65), channel_id=1, replica_groups=mesh['prefix'=16,'ctx'=4,'kvh'=8] {'ctx'}, use_global_device_ids=true, to_apply=%region_4.5 | all-reduce | flops 1024 | bytes 8192 | tf_op jit(solution)/shard_map/pmax | solution.py:55
  69.0 23.9 %while.25 = (s32[]{:T(128)}, f32[128,1,8,128]{0,3,2,1:T(8,128)S(1)}, f32[1,128,8]{1,2,0:T(8,128)S(1)}, bf16[8,512,1,128]{3,1,0,2:T(8,128)(2,1)}, bf16[8,512,1,12...) while((s32[]{:T(128)}, ...), condition=%wide.region_7.8_spmd.clone, body=%wide.region_5.7_spmd.clone.sunk | while | flops 271844352 | bytes 5792872 | solution.py:73
  69.0 1.4 bitcast_reduce_fusion.2
  70.4 1.5 fusion.29
  72.0 1.4 bitcast_reduce_fusion.2
  73.4 1.5 fusion.29
  75.0 1.4 bitcast_reduce_fusion.2
  76.4 1.5 fusion.29
  78.0 1.4 bitcast_reduce_fusion.2
  79.4 1.5 fusion.29
  80.9 1.4 bitcast_reduce_fusion.2
  82.4 1.5 fusion.29
  83.9 1.4 bitcast_reduce_fusion.2
  85.4 1.5 fusion.29
  86.9 1.4 bitcast_reduce_fusion.2
  88.4 1.5 fusion.29
  89.9 1.4 bitcast_reduce_fusion.2
  91.3 1.5 fusion.29
  92.9 1.0 copy.33
  93.9 0.1 reshape_transpose.3
  94.0 17.3 %psum.15 = f32[4,32,1,8]{1,0,3,2:T(4,128)S(1)} all-reduce(f32[4,32,1,8]{1,0,3,2:T(4,128)S(1)} %reshape_transpose.3), channel_id=1, replica_groups=mesh['prefix'=16,'ctx'=4,'kvh'=8] {'ctx'}, use_global_device_ids=true, to_apply=%region_9.10 | all-reduce | flops 1024 | bytes 8192 | tf_op jit(solution)/shard_map/psum | solution.py:77
  111.3 0.1 copy.34
  111.4 0.1 div.16
  111.5 0.1 div.17
  111.6 36.9 %all-reduce.2.cloned.1.call-done = f32[4,32,1,8,128]{4,3,1,0,2:T(8,128)} async-done(((f32[4,32,1,8,128]{4,3,1,0,2:T(8,128)}), f32[4,32,1,8,128]{4,3,1,0,2:T(8,128)}) %all-reduce.2.cloned.1.call-update) | async-done | bytes 524304 | tf_op jit(solution)/shard_map/psum | solution.py:77
  148.5 0.9 constant_dynamic-slice_fusion.1
  149.4 0.1 squeeze.11
  149.5 0.7 divide_convert_fusion
  150.2 6.9 %all-to-all-start.1 = ((bf16[16,2,1024]{2,1,0:T(2,128)(2,1)}), bf16[16,2,1024]{2,1,0:T(2,128)(2,1)S(1)}, u32[]{:S(2)}, u32[]{:S(2)}) async-start(bf16[16,2,1024]{2,1,0:T(2,128)(2,1)} %divide_convert_fusion), calls=%async_computation.1 | async-start | bytes 131072 | tf_op jit(solution)/shard_map/all_to_all | solution.py:84
  157.1 8.6 %all-to-all-done.1 = bf16[16,2,1024]{2,1,0:T(2,128)(2,1)S(1)} async-done(((bf16[16,2,1024]{2,1,0:T(2,128)(2,1)}), bf16[16,2,1024]{2,1,0:T(2,128)(2,1)S(1)}, u32[]{:S(2)}, u32[]{:S(2)}) %all-to-all-start.1) | async-done | bytes 65568 | tf_op jit(solution)/shard_map/all_to_all | solution.py:84
  165.7 0.8 convolution_convert_fusion.1
  (29 shorter events, 0.3 us)
Async XLA Ops:
  6.5 1.6 copy-start
  8.9 17.5 %all-to-all-start = ((bf16[16,2,1024]{2,1,0:T(2,128)(2,1)}), bf16[16,2,1024]{2,1,0:T(2,128)(2,1)S(1)}, u32[]{:S(2)}, u32[]{:S(2)}) async-start(bf16[16,2,1024]{2,1,0:T(2,128)(2,1)} %reshape.63), calls=%async_computation | async-start | bytes 131072 | tf_op jit(solution)/shard_map/all_to_all | solution.py:31
  17.9 130.6 %all-reduce.2.cloned.1.call-start = ((), (), s32[]{:S(2)}) async-start(), calls=%async_computation.2 | async-start | bytes 1048576 | tf_op jit(solution)/shard_map/psum | solution.py:77
  92.9 64.2 %copy-start.1 = (s32[16,1]{0,1:T(1,128)S(1)}, s32[16,1]{0,1:T(1,128)}, u32[]{:S(2)}) copy-start(s32[16,1]{0,1:T(1,128)} %param.9) | copy-start | bytes 196
  150.2 15.5 %all-to-all-start.1 = ((bf16[16,2,1024]{2,1,0:T(2,128)(2,1)}), bf16[16,2,1024]{2,1,0:T(2,128)(2,1)S(1)}, u32[]{:S(2)}, u32[]{:S(2)}) async-start(bf16[16,2,1024]{2,1,0:T(2,128)(2,1)} %divide_convert_fusion), calls=%async_computation.1 | async-start | bytes 131072 | tf_op jit(solution)/shard_map/all_to_all | solution.py:84
Sparse Core Ops, SparseCore 0:
  94.0 54.3 all-reduce.1
where the time goes:
time: 174 us; the launch traced here: 173 us
  waiting for transfers between devices  53.9 us (31%)
  blocking collectives  48.5 us (28%)
  matrix products  35.3 us (20%)
  starting transfers between devices  16 us (9%)
  between operations  13.5 us (8%)
  local copies, waits for them, and re-layouts  3.22 us (2%)
  other arithmetic  2.38 us (1%)
    psum x1, waiting for transfers between devices, body(): totals = lax.psum((numer_split, denom_split), 'ctx')  36.9 us
    dot_general x16, matrix products, block_scores(): jnp.einsum('sked,tkd->kset', queried, key_block, preferred_element_type=j...  22.3 us
    all_gather x1, blocking collectives, body(): group_rows = lax.all_gather(arrived[None], 'ctx', axis=0, tiled=True)  19.5 us
    psum x1, blocking collectives, body(): totals = lax.psum((numer_split, denom_split), 'ctx')  17.3 us
    dot_general x8, matrix products, sum_step(): jnp.einsum('kset,tkd->sked', expo.astype(jnp.bfloat16), blocks[1], prefer...  12 us
    pmax x1, blocking collectives, body(): row_max = lax.pmax(local_max, 'ctx')  11.7 us
    all_to_all x1, starting transfers between devices, body(): lax.all_to_all(outgoing, 'prefix', split_axis=0, concat_axis=0, tiled=True)  9.01 us
    all_to_all x1, waiting for transfers between devices, body(): lax.all_to_all(answer, 'prefix', split_axis=0, concat_axis=0, tiled=True)  8.55 us
  transfers between devices with their start and end apart: 3, of which 3 were waited for; matrix products, arithmetic and copies ran while one was open for 0% of the time, Pallas kernels for 0%

commit v1 on v0

v1 whole, which is shorter than its diff:
```python
import functools
import math

import jax
import jax.numpy as jnp
from jax import lax
from jax.experimental import pallas as pl
from jax.experimental.pallas import tpu as pltpu
from jax.sharding import PartitionSpec as P

DH = 128
SEND_CAP = 2
GROUP = 8
VMEM_LIMIT = 63 * 1024 * 1024
LANES = 128
PIECE = 512
N_CHUNKS = 4
MSG = SEND_CAP * GROUP


def iota(shape, dim):
    return lax.broadcasted_iota(jnp.int32, shape, dim)


def slot_targets(ids_ref):
    n_req = ids_ref.shape[1]
    lane_req = iota((n_req, LANES), 1) % n_req
    row_req = iota((n_req, LANES), 0)
    row = jnp.concatenate([ids_ref[...]] * (LANES // n_req), axis=1)
    col = jnp.sum(jnp.where(iota((n_req, LANES), 1) == row_req, row, 0), axis=1, keepdims=True)
    same = col == row
    rank_row = jnp.sum(jnp.where(same & (row_req < lane_req), 1, 0), axis=0, keepdims=True)
    first = iota((n_req, LANES), 1) < row_req
    rank_col = jnp.sum(jnp.where(same & first, 1, 0), axis=1, keepdims=True)
    return row * SEND_CAP + rank_row, col * SEND_CAP + rank_col


def prefix_order(n_pre):
    side = n_pre // 2
    fours = [[0, side, 1, -1]]
    rest = [[side + 1, side - 1, 2, -2]]
    for far in range(2, side // 2):
        rest.append([side + far, side - far, far + 1, -far - 1])
    rest[-1][-1] = side + side // 2
    order = [step % n_pre for four in fours + rest[1:] + rest[:1] for step in four]
    assert sorted(order) == list(range(n_pre))
    return order


def kernel(
    n_pre, n_ctx, block_len, queries_hbm, ids_hbm, keys, values, out,
    queries, ids, outgoing, q_in, k_raw, v_ones, scores, acc, part, stat, part_in, stat_in,
    load_sem, q_send, q_recv, part_send, part_recv, stat_send, stat_recv,
):
    n_req, features = queries.shape
    ctx_len = keys.shape[1]
    rows = n_pre * MSG
    chunk_rows = n_pre * n_ctx * MSG // N_CHUNKS
    per_tile = LANES // MSG
    pre = lax.axis_index("prefix")
    ctx = lax.axis_index("ctx")
    log_scale = DH ** (-0.5) * math.log2(math.e)

    kvh, n_kvh = lax.axis_index("kvh"), lax.axis_size("kvh")
    pre_at = [lax.rem(pre + step, n_pre) for step in range(n_pre)]
    pre_base = [to * (n_ctx * n_kvh) + kvh for to in pre_at]
    ctx_base = [lax.rem(ctx + off, n_ctx) * n_kvh for off in range(n_ctx)]

    order = prefix_order(n_pre)
    slots = [(step, off) for step in order for off in range(n_ctx)]
    n_slots = len(slots)
    per_chunk = n_slots // N_CHUNKS

    loads = [
        pltpu.make_async_copy(ids_hbm, ids, load_sem.at[2]),
        pltpu.make_async_copy(queries_hbm, queries, load_sem.at[3]),
        pltpu.make_async_copy(keys.at[0], k_raw, load_sem.at[0]),
        pltpu.make_async_copy(values.at[0], v_ones.at[:, pl.ds(0, DH)], load_sem.at[1]),
    ]
    for copy in loads:
        copy.start()
    barrier = pltpu.get_barrier_semaphore()

    for off in range(n_ctx):
        for step in range(n_pre):
            if off or step:
                pl.semaphore_signal(
                    barrier, inc=1, device_id=pre_base[step] + ctx_base[off], device_id_type=pl.DeviceIdType.LOGICAL
                )
    v_ones[:, DH:] = jnp.ones((ctx_len, DH), jnp.bfloat16)
    for copy in loads[:2]:
        copy.wait()

    target_row, target_col = slot_targets(ids)
    r = iota((rows, LANES), 0)
    lane = iota((rows, LANES), 1)
    place = (jnp.broadcast_to(target_row, (rows, LANES)) == r // GROUP) & (r % GROUP == lane // n_req)
    by_head = jnp.concatenate([queries[:, e * DH:(e + 1) * DH] for e in range(GROUP)], axis=0)
    outgoing[...] = jnp.dot(
        jnp.where(place, 1.0, 0.0).astype(jnp.bfloat16), by_head, preferred_element_type=jnp.float32
    ).astype(jnp.bfloat16).reshape(n_pre, MSG, DH)

    pl.semaphore_wait(barrier, n_pre * n_ctx - 1)

    pltpu.make_async_copy(outgoing.at[pre], q_in.at[0], q_recv.at[0]).start()
    for slot, (step, off) in enumerate(slots):
        if slot:
            back, away = (n_pre - step) % n_pre, (n_ctx - off) % n_ctx
            pltpu.make_async_remote_copy(
                src_ref=outgoing.at[pre_at[back]], dst_ref=q_in.at[slot], send_sem=q_send,
                recv_sem=q_recv.at[slot // per_chunk], device_id=pre_base[back] + ctx_base[away],
                device_id_type=pl.DeviceIdType.LOGICAL,
            ).start()
    for copy in loads[2:]:
        copy.wait()
    n_steps = ctx_len // block_len

    def chunk_step(chunk, carry):
        mine = pl.ds(pl.multiple_of(chunk * per_chunk, per_chunk), per_chunk)
        pltpu.make_async_copy(q_in.at[mine], q_in.at[mine], q_recv.at[chunk]).wait()
        q = q_in[mine].reshape(chunk_rows, DH)

        def score_step(j, top):
            for piece in range(block_len // PIECE):
                span = pl.ds(pl.multiple_of(j * block_len + piece * PIECE, PIECE), PIECE)
                s = lax.dot_general(q, k_raw[span, :], (((1,), (1,)), ((), ())), preferred_element_type=jnp.float32)
                scores[:, span] = s
                for i in range(PIECE // LANES):
                    top = jnp.maximum(top, s[:, i * LANES:(i + 1) * LANES])
            return top

        top = lax.fori_loop(0, n_steps, score_step, jnp.full((chunk_rows, LANES), -jnp.inf, jnp.float32))
        top = jnp.max(top, axis=1, keepdims=True) * log_scale
        acc[...] = jnp.zeros(acc.shape, jnp.float32)

        def weight_step(j, carry):
            added = None
            for piece in range(block_len // PIECE):
                span = pl.ds(pl.multiple_of(j * block_len + piece * PIECE, PIECE), PIECE)
                p = jnp.exp2(scores[:, span] * log_scale - top).astype(jnp.bfloat16)
                more = jnp.dot(p, v_ones[span, :], preferred_element_type=jnp.float32)
                added = more if added is None else added + more
            acc[...] += added
            return carry

        lax.fori_loop(0, n_steps, weight_step, 0)
        denom = acc[:, DH:]
        lse = top + jnp.log2(denom)
        part[mine] = (acc[:, :DH] / denom).astype(jnp.bfloat16).reshape(per_chunk, MSG, DH)
        own_lanes = iota((LANES, LANES), 1) == lax.rem(pre, per_tile) * MSG + iota((LANES, LANES), 0) % MSG
        for h in range(chunk_rows // LANES):
            spread = jnp.where(own_lanes, lse[h * LANES:(h + 1) * LANES], 0.0)
            stat[pl.ds(pl.multiple_of(chunk * per_chunk + h * per_tile, per_tile), per_tile)] = jnp.sum(
                spread.reshape(per_tile, MSG, LANES), axis=1, keepdims=True
            )

        def send_parts(which):
            for slot in range(which * per_chunk, (which + 1) * per_chunk):
                step, off = slots[slot]
                if slot == 0:
                    pltpu.make_async_copy(part.at[0], part_in.at[0, pre], part_recv).start()
                    pltpu.make_async_copy(stat.at[0], stat_in.at[0, pre], stat_recv).start()
                    continue
                for src, dst, send_sem, recv_sem in (
                    (part, part_in, part_send, part_recv), (stat, stat_in, stat_send, stat_recv)
                ):
                    pltpu.make_async_remote_copy(
                        src_ref=src.at[slot], dst_ref=dst.at[off, pre], send_sem=send_sem, recv_sem=recv_sem,
                        device_id=pre_base[step] + ctx_base[off], device_id_type=pl.DeviceIdType.LOGICAL,
                    ).start()

        for which in range(N_CHUNKS):
            pl.when(chunk == which)(functools.partial(send_parts, which))
        return carry

    lax.fori_loop(0, N_CHUNKS, chunk_step, 0)

    targets = jnp.concatenate([target_col] * GROUP, axis=0)
    r = iota((GROUP * n_req, rows), 0)
    lane = iota((GROUP * n_req, rows), 1)
    pick = (targets == lane // GROUP) & (r // n_req == lane % GROUP)
    pltpu.make_async_copy(stat_in, stat_in, stat_recv).wait()
    lses = [
        jnp.concatenate([
            jnp.sum(stat_in[chunk, h * per_tile:(h + 1) * per_tile], axis=0) for h in range(rows // LANES)
        ], axis=1)
        for chunk in range(n_ctx)
    ]
    highest = functools.reduce(jnp.maximum, lses)
    shares = [jnp.exp2(lse - highest) for lse in lses]
    total = functools.reduce(jnp.add, shares)
    pltpu.make_async_copy(part_in, part_in, part_recv).wait()
    answer = None
    for chunk in range(n_ctx):
        weight = jnp.where(pick, shares[chunk] / total, 0.0)
        coarse = weight.astype(jnp.bfloat16)
        fine = (weight - coarse.astype(jnp.float32)).astype(jnp.bfloat16)
        arrived = part_in[chunk].reshape(rows, DH)
        for term in (coarse, fine):
            more = jnp.dot(term, arrived, preferred_element_type=jnp.float32)
            answer = more if answer is None else answer + more
    answer = answer.astype(jnp.bfloat16)
    for e in range(GROUP):
        out[:, e * DH:(e + 1) * DH] = answer[e * n_req:(e + 1) * n_req]

    def sent(ref, sem):
        pltpu.make_async_copy(ref.at[pl.ds(1, n_slots - 1)], ref.at[pl.ds(1, n_slots - 1)], sem).wait()

    sent(q_in, q_send)
    sent(part, part_send)
    sent(stat, stat_send)


def body(queries, prefix_ids, keys, values):
    n_pre = lax.axis_size("prefix")
    n_ctx = lax.axis_size("ctx")
    ctx_len = keys.shape[1]
    rows = n_pre * MSG
    n_slots = n_pre * n_ctx
    chunk_rows = n_slots * MSG // N_CHUNKS
    block_len = min(2048, ctx_len)
    f32, bf16 = jnp.float32, jnp.bfloat16
    vmem = pl.BlockSpec(memory_space=pltpu.VMEM)
    hbm = pl.BlockSpec(memory_space=pl.ANY)
    dma = pltpu.SemaphoreType.DMA
    return pl.pallas_call(
        functools.partial(kernel, n_pre, n_ctx, block_len),
        out_shape=jax.ShapeDtypeStruct(queries.shape, bf16),
        in_specs=[hbm, hbm, hbm, hbm],
        out_specs=vmem,
        scratch_shapes=[
            pltpu.VMEM(queries.shape, bf16),
            pltpu.VMEM((1, queries.shape[0]), jnp.int32),
            pltpu.VMEM((n_pre, MSG, DH), bf16),
            pltpu.VMEM((n_slots, MSG, DH), bf16),
            pltpu.VMEM((ctx_len, DH), bf16),
            pltpu.VMEM((ctx_len, 2 * DH), bf16),
            pltpu.VMEM((chunk_rows, ctx_len), f32),
            pltpu.VMEM((chunk_rows, 2 * DH), f32),
            pltpu.VMEM((n_slots, MSG, DH), bf16),
            pltpu.VMEM((n_slots, 1, LANES), f32),
            pltpu.VMEM((n_ctx, n_pre, MSG, DH), bf16),
            pltpu.VMEM((n_ctx, n_pre, 1, LANES), f32),
            dma((4,)), dma, dma((N_CHUNKS,)), dma, dma, dma, dma,
        ],
        compiler_params=pltpu.CompilerParams(
            collective_id=0, has_side_effects=True, vmem_limit_bytes=VMEM_LIMIT
        ),
        cost_estimate=pl.CostEstimate(
            flops=4 * n_ctx * rows * ctx_len * DH, bytes_accessed=4 * ctx_len * DH,
            transcendentals=n_ctx * rows * ctx_len,
        ),
    )(queries, prefix_ids.reshape(1, -1), keys, values)


def solution(mesh):
    in_specs = (
        P(("prefix", "ctx"), "kvh"),
        P(("prefix", "ctx"), None),
        P("prefix", "ctx", "kvh"),
        P("prefix", "ctx", "kvh"),
    )
    out_specs = P(("prefix", "ctx"), "kvh")
    return jax.shard_map(body, mesh=mesh, in_specs=in_specs, out_specs=out_specs, check_vma=False)
```

time: 174 us -> 39.7 us (0.23)
  the two profiles are of different devices: /device:TPU:2 before, /device:TPU:20 now
where the time goes in v1:
time: 39.7 us; the launch traced here: 39.5 us
  Pallas kernels  38.1 us (96%)
  local copies, waits for them, and re-layouts  1.38 us (3%)
    pallas_call x1, Pallas kernels, body(): pl.pallas_call(functools.partial(kernel, n_pre, n_ctx, block_len), out_sh...  38.1 us
    unnamed x1, local copies, waits for them, and re-layouts  1.38 us

profile of v1, /device:TPU:20, one launch (start us, length us, event | category | flops | bytes accessed | tf_op | source)
XLA Modules:
  0.0 39.5 jit_solution(15242485641984856822)
XLA Ops:
  0.0 38.1 %shard_map.46 = bf16[16,1024]{1,0:T(8,128)(2,1)} custom-call(bf16[16,1024]{1,0:T(8,128)(2,1)} %queries_hbm.1, s32[1,16]{1,0:T(1,128)} %bitcast.1, bf16[1,4096,128]{2,1,0:T(8,128)(2,1)} %keys.1, bf16[1,4096,128]{2,1,0:T(8,128)(2,1)} %values.1), custom_call_target="tpu_custom_call" | custom-call | flops 2147483648 | bytes 2097152 | tf_op jit(solution)/shard_map/pallas_call | solution.py:226
  38.1 1.4 %copy.6 = bf16[16,1024]{1,0:T(8,128)(2,1)} copy(bf16[16,1024]{1,0:T(8,128)(2,1)} %shard_map.46) | data formatting | bytes 65536

commit v2 on v1

--- a/solution.py
+++ b/solution.py
@@ -50,7 +50,7 @@
 def kernel(
     n_pre, n_ctx, block_len, queries_hbm, ids_hbm, keys, values, out,
     queries, ids, outgoing, q_in, k_raw, v_ones, scores, acc, part, stat, part_in, stat_in,
-    load_sem, q_send, q_recv, part_send, part_recv, stat_send, stat_recv,
+    plane_sem, load_sem, q_send, q_recv, part_send, part_recv, stat_send, stat_recv,
 ):
     n_req, features = queries.shape
     ctx_len = keys.shape[1]
@@ -67,7 +67,8 @@
     ctx_base = [lax.rem(ctx + off, n_ctx) * n_kvh for off in range(n_ctx)]
 
     order = prefix_order(n_pre)
-    slots = [(step, off) for step in order for off in range(n_ctx)]
+    near = [(step, 0) for step in order]
+    slots = near + [(step, off) for step in order for off in (1, n_ctx - 1, 2)]
     n_slots = len(slots)
     per_chunk = n_slots // N_CHUNKS
 
@@ -81,13 +82,14 @@
         copy.start()
     barrier = pltpu.get_barrier_semaphore()
 
-    for off in range(n_ctx):
-        for step in range(n_pre):
-            if off or step:
-                pl.semaphore_signal(
-                    barrier, inc=1, device_id=pre_base[step] + ctx_base[off], device_id_type=pl.DeviceIdType.LOGICAL
-                )
-    v_ones[:, DH:] = jnp.ones((ctx_len, DH), jnp.bfloat16)
+    for off in range(1, n_ctx):
+        pl.semaphore_signal(
+            barrier, inc=1, device_id=pre_base[0] + ctx_base[off], device_id_type=pl.DeviceIdType.LOGICAL
+        )
+    for step in order[1:]:
+        pl.semaphore_signal(
+            barrier, inc=1, device_id=pre_base[step] + ctx_base[0], device_id_type=pl.DeviceIdType.LOGICAL
+        )
     for copy in loads[:2]:
         copy.wait()
 
@@ -100,17 +102,28 @@
         jnp.where(place, 1.0, 0.0).astype(jnp.bfloat16), by_head, preferred_element_type=jnp.float32
     ).astype(jnp.bfloat16).reshape(n_pre, MSG, DH)
 
-    pl.semaphore_wait(barrier, n_pre * n_ctx - 1)
-
-    pltpu.make_async_copy(outgoing.at[pre], q_in.at[0], q_recv.at[0]).start()
-    for slot, (step, off) in enumerate(slots):
-        if slot:
+    pl.semaphore_wait(barrier, n_pre - 1 + n_ctx - 1)
+    for off in range(1, n_ctx):
+        pl.semaphore_signal(
+            plane_sem, inc=1, device_id=pre_base[0] + ctx_base[off], device_id_type=pl.DeviceIdType.LOGICAL
+        )
+
+    def send_queries(first, last):
+        for slot in range(first, last):
+            step, off = slots[slot]
             back, away = (n_pre - step) % n_pre, (n_ctx - off) % n_ctx
             pltpu.make_async_remote_copy(
                 src_ref=outgoing.at[pre_at[back]], dst_ref=q_in.at[slot], send_sem=q_send,
                 recv_sem=q_recv.at[slot // per_chunk], device_id=pre_base[back] + ctx_base[away],
                 device_id_type=pl.DeviceIdType.LOGICAL,
             ).start()
+
+    pltpu.make_async_copy(outgoing.at[pre], q_in.at[0], q_recv.at[0]).start()
+    send_queries(1, n_pre)
+    v_ones[:, DH:] = jnp.ones((ctx_len, DH), jnp.bfloat16)
+
+    pl.semaphore_wait(plane_sem, n_ctx - 1)
+    send_queries(n_pre, n_slots)
     for copy in loads[2:]:
         copy.wait()
     n_steps = ctx_len // block_len
@@ -241,7 +254,7 @@
             pltpu.VMEM((n_slots, 1, LANES), f32),
             pltpu.VMEM((n_ctx, n_pre, MSG, DH), bf16),
             pltpu.VMEM((n_ctx, n_pre, 1, LANES), f32),
-            dma((4,)), dma, dma((N_CHUNKS,)), dma, dma, dma, dma,
+            pltpu.SemaphoreType.REGULAR, dma((4,)), dma, dma((N_CHUNKS,)), dma, dma, dma, dma,
         ],
         compiler_params=pltpu.CompilerParams(
             collective_id=0, has_side_effects=True, vmem_limit_bytes=VMEM_LIMIT

time: 39.7 us -> 40 us (level)
  the two profiles are of different devices: /device:TPU:20 before, /device:TPU:1 now
where the time goes in v2:
time: 40 us; the launch traced here: 39.8 us
  Pallas kernels  38.4 us (96%)
  local copies, waits for them, and re-layouts  1.38 us (3%)
    pallas_call x1, Pallas kernels, body(): pl.pallas_call(functools.partial(kernel, n_pre, n_ctx, block_len), out_sh...  38.4 us
    unnamed x1, local copies, waits for them, and re-layouts  1.38 us

profile of v2, /device:TPU:1, one launch (start us, length us, event | category | flops | bytes accessed | tf_op | source)
XLA Modules:
  0.0 39.8 jit_solution(4200711068266754028)
XLA Ops:
  0.0 38.4 %shard_map.46 = bf16[16,1024]{1,0:T(8,128)(2,1)} custom-call(bf16[16,1024]{1,0:T(8,128)(2,1)} %queries_hbm.1, s32[1,16]{1,0:T(1,128)} %bitcast.1, bf16[1,4096,128]{2,1,0:T(8,128)(2,1)} %keys.1, bf16[1,4096,128]{2,1,0:T(8,128)(2,1)} %values.1), custom_call_target="tpu_custom_call" | custom-call | flops 2147483648 | bytes 2097152 | tf_op jit(solution)/shard_map/pallas_call | solution.py:239
  38.4 1.4 %copy.6 = bf16[16,1024]{1,0:T(8,128)(2,1)} copy(bf16[16,1024]{1,0:T(8,128)(2,1)} %shard_map.46) | data formatting | bytes 65536

commit v3 on v1

--- a/solution.py
+++ b/solution.py
@@ -14,7 +14,6 @@
 VMEM_LIMIT = 63 * 1024 * 1024
 LANES = 128
 PIECE = 512
-N_CHUNKS = 4
 MSG = SEND_CAP * GROUP
 
 
@@ -35,27 +34,14 @@
     return row * SEND_CAP + rank_row, col * SEND_CAP + rank_col
 
 
-def prefix_order(n_pre):
-    side = n_pre // 2
-    fours = [[0, side, 1, -1]]
-    rest = [[side + 1, side - 1, 2, -2]]
-    for far in range(2, side // 2):
-        rest.append([side + far, side - far, far + 1, -far - 1])
-    rest[-1][-1] = side + side // 2
-    order = [step % n_pre for four in fours + rest[1:] + rest[:1] for step in four]
-    assert sorted(order) == list(range(n_pre))
-    return order
-
-
 def kernel(
     n_pre, n_ctx, block_len, queries_hbm, ids_hbm, keys, values, out,
     queries, ids, outgoing, q_in, k_raw, v_ones, scores, acc, part, stat, part_in, stat_in,
-    load_sem, q_send, q_recv, part_send, part_recv, stat_send, stat_recv,
+    ready_low, ready_high, load_sem, q_send, q_recv, part_send, part_recv, stat_send, stat_recv,
 ):
     n_req, features = queries.shape
     ctx_len = keys.shape[1]
     rows = n_pre * MSG
-    chunk_rows = n_pre * n_ctx * MSG // N_CHUNKS
     per_tile = LANES // MSG
     pre = lax.axis_index("prefix")
     ctx = lax.axis_index("ctx")
@@ -64,12 +50,50 @@
     kvh, n_kvh = lax.axis_index("kvh"), lax.axis_size("kvh")
     pre_at = [lax.rem(pre + step, n_pre) for step in range(n_pre)]
     pre_base = [to * (n_ctx * n_kvh) + kvh for to in pre_at]
-    ctx_base = [lax.rem(ctx + off, n_ctx) * n_kvh for off in range(n_ctx)]
-
-    order = prefix_order(n_pre)
-    slots = [(step, off) for step in order for off in range(n_ctx)]
-    n_slots = len(slots)
-    per_chunk = n_slots // N_CHUNKS
+    rank = ctx * n_pre + pre
+    half_len = n_pre // 2
+    ready = (ready_low, ready_high)
+
+    def in_half(index, half):
+        return index >= half_len if half else index < half_len
+
+    def device(step, to_ctx):
+        return pre_base[step % n_pre] + to_ctx * n_kvh
+
+    def later_ones(to_ctx, act):
+        @pl.when(to_ctx > ctx)
+        def _():
+            for step in range(1, n_pre + 1):
+                act(step)
+
+        @pl.when(to_ctx == ctx)
+        def _():
+            for step in range(1, n_pre):
+                pl.when(pre + step < n_pre)(functools.partial(act, step))
+
+    def earlier_ones(to_ctx, act):
+        @pl.when(to_ctx < ctx)
+        def _():
+            for step in range(1, n_pre + 1):
+                act(n_pre - step)
+
+        @pl.when(to_ctx == ctx)
+        def _():
+            for step in range(1, n_pre):
+                pl.when(pre >= step)(functools.partial(act, n_pre - step))
+
+    def over_planes(first, last, loop, act):
+        def plane(to_ctx, carry):
+            loop(to_ctx, functools.partial(act, to_ctx))
+            return carry
+
+        lax.fori_loop(first, last, plane, 0)
+
+    def send_query(to_ctx, step):
+        pltpu.make_async_remote_copy(
+            src_ref=outgoing.at[pre_at[step % n_pre]], dst_ref=q_in.at[ctx, pre], send_sem=q_send, recv_sem=q_recv.at[ctx],
+            device_id=device(step, to_ctx), device_id_type=pl.DeviceIdType.LOGICAL,
+        ).start()
 
     loads = [
         pltpu.make_async_copy(ids_hbm, ids, load_sem.at[2]),
@@ -81,13 +105,21 @@
         copy.start()
     barrier = pltpu.get_barrier_semaphore()
 
-    for off in range(n_ctx):
-        for step in range(n_pre):
-            if off or step:
-                pl.semaphore_signal(
-                    barrier, inc=1, device_id=pre_base[step] + ctx_base[off], device_id_type=pl.DeviceIdType.LOGICAL
-                )
-    v_ones[:, DH:] = jnp.ones((ctx_len, DH), jnp.bfloat16)
+    over_planes(ctx, n_ctx, later_ones, lambda to_ctx, step: pl.semaphore_signal(
+        barrier, inc=1, device_id=device(step, to_ctx), device_id_type=pl.DeviceIdType.LOGICAL
+    ))
+
+    @pl.when(rank > 0)
+    def _():
+        pl.semaphore_wait(barrier, rank)
+
+    for half in range(2):
+        @pl.when(in_half(pre, half))
+        def _():
+            over_planes(0, ctx + 1, earlier_ones, lambda to_ctx, step: pl.semaphore_signal(
+                ready[half].at[ctx], inc=1, device_id=device(step, to_ctx), device_id_type=pl.DeviceIdType.LOGICAL
+            ))
+
     for copy in loads[:2]:
         copy.wait()
 
@@ -100,25 +132,40 @@
         jnp.where(place, 1.0, 0.0).astype(jnp.bfloat16), by_head, preferred_element_type=jnp.float32
     ).astype(jnp.bfloat16).reshape(n_pre, MSG, DH)
 
-    pl.semaphore_wait(barrier, n_pre * n_ctx - 1)
-
-    pltpu.make_async_copy(outgoing.at[pre], q_in.at[0], q_recv.at[0]).start()
-    for slot, (step, off) in enumerate(slots):
-        if slot:
-            back, away = (n_pre - step) % n_pre, (n_ctx - off) % n_ctx
-            pltpu.make_async_remote_copy(
-                src_ref=outgoing.at[pre_at[back]], dst_ref=q_in.at[slot], send_sem=q_send,
-                recv_sem=q_recv.at[slot // per_chunk], device_id=pre_base[back] + ctx_base[away],
-                device_id_type=pl.DeviceIdType.LOGICAL,
-            ).start()
+    pltpu.make_async_copy(outgoing.at[pre], q_in.at[ctx, pre], q_recv.at[ctx]).start()
+    over_planes(0, ctx + 1, earlier_ones, send_query)
+    v_ones[:, DH:] = jnp.ones((ctx_len, DH), jnp.bfloat16)
+
+    def serve(to_ctx, carry):
+        for half in range(2):
+            whole = to_ctx > ctx
+            if half:
+                whole = whole | ((to_ctx == ctx) & in_half(pre, 0))
+            later = (half + 1) * half_len - 1 - pre
+
+            @pl.when(whole)
+            def _():
+                pl.semaphore_wait(ready[half].at[to_ctx], half_len)
+                for step in range(1, n_pre + 1):
+                    pl.when(in_half(pre_at[step % n_pre], half))(functools.partial(send_query, to_ctx, step))
+
+            @pl.when((to_ctx == ctx) & in_half(pre, half) & (later > 0))
+            def _():
+                pl.semaphore_wait(ready[half].at[to_ctx], later)
+                for step in range(1, half_len):
+                    pl.when(pre + step < (half + 1) * half_len)(functools.partial(send_query, to_ctx, step))
+
+        return carry
+
+    lax.fori_loop(0, n_ctx, serve, 0)
     for copy in loads[2:]:
         copy.wait()
+    own_lanes = iota((LANES, LANES), 1) == lax.rem(pre, per_tile) * MSG + iota((LANES, LANES), 0) % MSG
     n_steps = ctx_len // block_len
 
     def chunk_step(chunk, carry):
-        mine = pl.ds(pl.multiple_of(chunk * per_chunk, per_chunk), per_chunk)
-        pltpu.make_async_copy(q_in.at[mine], q_in.at[mine], q_recv.at[chunk]).wait()
-        q = q_in[mine].reshape(chunk_rows, DH)
+        pltpu.make_async_copy(q_in.at[chunk], q_in.at[chunk], q_recv.at[chunk]).wait()
+        q = q_in[chunk].reshape(rows, DH)
 
         def score_step(j, top):
             for piece in range(block_len // PIECE):
@@ -129,7 +176,7 @@
                     top = jnp.maximum(top, s[:, i * LANES:(i + 1) * LANES])
             return top
 
-        top = lax.fori_loop(0, n_steps, score_step, jnp.full((chunk_rows, LANES), -jnp.inf, jnp.float32))
+        top = lax.fori_loop(0, n_steps, score_step, jnp.full((rows, LANES), -jnp.inf, jnp.float32))
         top = jnp.max(top, axis=1, keepdims=True) * log_scale
         acc[...] = jnp.zeros(acc.shape, jnp.float32)
 
@@ -146,34 +193,37 @@
         lax.fori_loop(0, n_steps, weight_step, 0)
         denom = acc[:, DH:]
         lse = top + jnp.log2(denom)
-        part[mine] = (acc[:, :DH] / denom).astype(jnp.bfloat16).reshape(per_chunk, MSG, DH)
-        own_lanes = iota((LANES, LANES), 1) == lax.rem(pre, per_tile) * MSG + iota((LANES, LANES), 0) % MSG
-        for h in range(chunk_rows // LANES):
+        part[chunk] = (acc[:, :DH] / denom).astype(jnp.bfloat16).reshape(n_pre, MSG, DH)
+        for h in range(rows // LANES):
             spread = jnp.where(own_lanes, lse[h * LANES:(h + 1) * LANES], 0.0)
-            stat[pl.ds(pl.multiple_of(chunk * per_chunk + h * per_tile, per_tile), per_tile)] = jnp.sum(
+            stat[chunk, h * per_tile:(h + 1) * per_tile] = jnp.sum(
                 spread.reshape(per_tile, MSG, LANES), axis=1, keepdims=True
             )
 
-        def send_parts(which):
-            for slot in range(which * per_chunk, (which + 1) * per_chunk):
-                step, off = slots[slot]
-                if slot == 0:
-                    pltpu.make_async_copy(part.at[0], part_in.at[0, pre], part_recv).start()
-                    pltpu.make_async_copy(stat.at[0], stat_in.at[0, pre], stat_recv).start()
-                    continue
-                for src, dst, send_sem, recv_sem in (
-                    (part, part_in, part_send, part_recv), (stat, stat_in, stat_send, stat_recv)
-                ):
-                    pltpu.make_async_remote_copy(
-                        src_ref=src.at[slot], dst_ref=dst.at[off, pre], send_sem=send_sem, recv_sem=recv_sem,
-                        device_id=pre_base[step] + ctx_base[off], device_id_type=pl.DeviceIdType.LOGICAL,
-                    ).start()
-
-        for which in range(N_CHUNKS):
-            pl.when(chunk == which)(functools.partial(send_parts, which))
+        def send_part(step):
+            to = pre_at[step]
+            for src, dst, send_sem, recv_sem in (
+                (part, part_in, part_send, part_recv), (stat, stat_in, stat_send, stat_recv)
+            ):
+                pltpu.make_async_remote_copy(
+                    src_ref=src.at[chunk, to], dst_ref=dst.at[ctx, pre], send_sem=send_sem, recv_sem=recv_sem,
+                    device_id=device(step, chunk), device_id_type=pl.DeviceIdType.LOGICAL,
+                ).start()
+
+        @pl.when(chunk == ctx)
+        def _():
+            pltpu.make_async_copy(part.at[chunk, pre], part_in.at[ctx, pre], part_recv).start()
+            pltpu.make_async_copy(stat.at[chunk, pre], stat_in.at[ctx, pre], stat_recv).start()
+
+        @pl.when(chunk != ctx)
+        def _():
+            send_part(0)
+
+        for step in range(1, n_pre):
+            send_part(step)
         return carry
 
-    lax.fori_loop(0, N_CHUNKS, chunk_step, 0)
+    lax.fori_loop(0, n_ctx, chunk_step, 0)
 
     targets = jnp.concatenate([target_col] * GROUP, axis=0)
     r = iota((GROUP * n_req, rows), 0)
@@ -204,7 +254,8 @@
         out[:, e * DH:(e + 1) * DH] = answer[e * n_req:(e + 1) * n_req]
 
     def sent(ref, sem):
-        pltpu.make_async_copy(ref.at[pl.ds(1, n_slots - 1)], ref.at[pl.ds(1, n_slots - 1)], sem).wait()
+        pltpu.make_async_copy(ref.at[pl.ds(1, n_ctx - 1)], ref.at[pl.ds(1, n_ctx - 1)], sem).wait()
+        pltpu.make_async_copy(ref.at[0, pl.ds(1, n_pre - 1)], ref.at[0, pl.ds(1, n_pre - 1)], sem).wait()
 
     sent(q_in, q_send)
     sent(part, part_send)
@@ -216,8 +267,6 @@
     n_ctx = lax.axis_size("ctx")
     ctx_len = keys.shape[1]
     rows = n_pre * MSG
-    n_slots = n_pre * n_ctx
-    chunk_rows = n_slots * MSG // N_CHUNKS
     block_len = min(2048, ctx_len)
     f32, bf16 = jnp.float32, jnp.bfloat16
     vmem = pl.BlockSpec(memory_space=pltpu.VMEM)
@@ -232,16 +281,16 @@
             pltpu.VMEM(queries.shape, bf16),
             pltpu.VMEM((1, queries.shape[0]), jnp.int32),
             pltpu.VMEM((n_pre, MSG, DH), bf16),
-            pltpu.VMEM((n_slots, MSG, DH), bf16),
+            pltpu.VMEM((n_ctx, n_pre, MSG, DH), bf16),
             pltpu.VMEM((ctx_len, DH), bf16),
             pltpu.VMEM((ctx_len, 2 * DH), bf16),
-            pltpu.VMEM((chunk_rows, ctx_len), f32),
-            pltpu.VMEM((chunk_rows, 2 * DH), f32),
-            pltpu.VMEM((n_slots, MSG, DH), bf16),
-            pltpu.VMEM((n_slots, 1, LANES), f32),
+            pltpu.VMEM((rows, ctx_len), f32),
+            pltpu.VMEM((rows, 2 * DH), f32),
             pltpu.VMEM((n_ctx, n_pre, MSG, DH), bf16),
             pltpu.VMEM((n_ctx, n_pre, 1, LANES), f32),
-            dma((4,)), dma, dma((N_CHUNKS,)), dma, dma, dma, dma,
+            pltpu.VMEM((n_ctx, n_pre, MSG, DH), bf16),
+            pltpu.VMEM((n_ctx, n_pre, 1, LANES), f32),
+            pltpu.SemaphoreType.REGULAR((n_ctx,)), pltpu.SemaphoreType.REGULAR((n_ctx,)), dma((4,)), dma, dma((n_ctx,)), dma, dma, dma, dma,
         ],
         compiler_params=pltpu.CompilerParams(
             collective_id=0, has_side_effects=True, vmem_limit_bytes=VMEM_LIMIT

time: 39.7 us -> 39 us (0.982)
  the two profiles are of different devices: /device:TPU:20 before, /device:TPU:132 now
where the time goes in v3:
time: 39 us; the launch traced here: 38.9 us
  Pallas kernels  37.5 us (96%)
  local copies, waits for them, and re-layouts  1.38 us (4%)
    pallas_call x1, Pallas kernels, body(): pl.pallas_call(functools.partial(kernel, n_pre, n_ctx, block_len), out_sh...  37.5 us
    unnamed x1, local copies, waits for them, and re-layouts  1.38 us

profile of v3, /device:TPU:132, one launch (start us, length us, event | category | flops | bytes accessed | tf_op | source)
XLA Modules:
  0.0 38.9 jit_solution(14104316856075879981)
XLA Ops:
  0.0 37.5 %shard_map.46 = bf16[16,1024]{1,0:T(8,128)(2,1)} custom-call(bf16[16,1024]{1,0:T(8,128)(2,1)} %queries_hbm.1, s32[1,16]{1,0:T(1,128)} %bitcast.1, bf16[1,4096,128]{2,1,0:T(8,128)(2,1)} %keys.1, bf16[1,4096,128]{2,1,0:T(8,128)(2,1)} %values.1), custom_call_target="tpu_custom_call" | custom-call | flops 2147483648 | bytes 2097152 | tf_op jit(solution)/shard_map/pallas_call | solution.py:275
  37.5 1.4 %copy.6 = bf16[16,1024]{1,0:T(8,128)(2,1)} copy(bf16[16,1024]{1,0:T(8,128)(2,1)} %shard_map.46) | data formatting | bytes 65536

commit v4 on v3

--- a/solution.py
+++ b/solution.py
@@ -267,7 +267,7 @@
     n_ctx = lax.axis_size("ctx")
     ctx_len = keys.shape[1]
     rows = n_pre * MSG
-    block_len = min(2048, ctx_len)
+    block_len = min(1024, ctx_len)
     f32, bf16 = jnp.float32, jnp.bfloat16
     vmem = pl.BlockSpec(memory_space=pltpu.VMEM)
     hbm = pl.BlockSpec(memory_space=pl.ANY)

time: 39 us -> 40.7 us (1.044)
  Pallas kernels: 37.5 us -> 39.2 us
    pallas_call x1, Pallas kernels: 37.5 us -> 39.2 us  [body(): pl.pallas_call(functools.partial(kernel, n_pre, n_ctx, block_len), out_sh...]
where the time goes in v4:
time: 40.7 us; the launch traced here: 40.5 us
  Pallas kernels  39.2 us (96%)
  local copies, waits for them, and re-layouts  1.38 us (3%)
    pallas_call x1, Pallas kernels, body(): pl.pallas_call(functools.partial(kernel, n_pre, n_ctx, block_len), out_sh...  39.2 us
    unnamed x1, local copies, waits for them, and re-layouts  1.38 us

profile of v4, /device:TPU:132, one launch (start us, length us, event | category | flops | bytes accessed | tf_op | source)
XLA Modules:
  0.0 40.5 jit_solution(12690641189064646866)
XLA Ops:
  0.0 39.2 %shard_map.46 = bf16[16,1024]{1,0:T(8,128)(2,1)} custom-call(bf16[16,1024]{1,0:T(8,128)(2,1)} %queries_hbm.1, s32[1,16]{1,0:T(1,128)} %bitcast.1, bf16[1,4096,128]{2,1,0:T(8,128)(2,1)} %keys.1, bf16[1,4096,128]{2,1,0:T(8,128)(2,1)} %values.1), custom_call_target="tpu_custom_call" | custom-call | flops 2147483648 | bytes 2097152 | tf_op jit(solution)/shard_map/pallas_call | solution.py:275
  39.2 1.4 %copy.6 = bf16[16,1024]{1,0:T(8,128)(2,1)} copy(bf16[16,1024]{1,0:T(8,128)(2,1)} %shard_map.46) | data formatting | bytes 65536

commit v5 on v3

--- a/solution.py
+++ b/solution.py
@@ -167,16 +167,13 @@
         pltpu.make_async_copy(q_in.at[chunk], q_in.at[chunk], q_recv.at[chunk]).wait()
         q = q_in[chunk].reshape(rows, DH)
 
-        def score_step(j, top):
-            for piece in range(block_len // PIECE):
-                span = pl.ds(pl.multiple_of(j * block_len + piece * PIECE, PIECE), PIECE)
-                s = lax.dot_general(q, k_raw[span, :], (((1,), (1,)), ((), ())), preferred_element_type=jnp.float32)
-                scores[:, span] = s
-                for i in range(PIECE // LANES):
-                    top = jnp.maximum(top, s[:, i * LANES:(i + 1) * LANES])
-            return top
-
-        top = lax.fori_loop(0, n_steps, score_step, jnp.full((rows, LANES), -jnp.inf, jnp.float32))
+        top = jnp.full((rows, LANES), -jnp.inf, jnp.float32)
+        for piece in range(ctx_len // PIECE):
+            span = slice(piece * PIECE, (piece + 1) * PIECE)
+            s = lax.dot_general(q, k_raw[span], (((1,), (1,)), ((), ())), preferred_element_type=jnp.float32)
+            scores[:, span] = s
+            for i in range(PIECE // LANES):
+                top = jnp.maximum(top, s[:, i * LANES:(i + 1) * LANES])
         top = jnp.max(top, axis=1, keepdims=True) * log_scale
         acc[...] = jnp.zeros(acc.shape, jnp.float32)
 

time: 39 us -> 38.7 us (level)
  the two profiles are of different devices: /device:TPU:132 before, /device:TPU:130 now
where the time goes in v5:
time: 38.7 us; the launch traced here: 38.5 us
  Pallas kernels  37.1 us (96%)
  local copies, waits for them, and re-layouts  1.38 us (4%)
    pallas_call x1, Pallas kernels, body(): pl.pallas_call(functools.partial(kernel, n_pre, n_ctx, block_len), out_sh...  37.1 us
    unnamed x1, local copies, waits for them, and re-layouts  1.38 us

profile of v5, /device:TPU:130, one launch (start us, length us, event | category | flops | bytes accessed | tf_op | source)
XLA Modules:
  0.0 38.5 jit_solution(6294729806018169840)
XLA Ops:
  0.0 37.1 %shard_map.46 = bf16[16,1024]{1,0:T(8,128)(2,1)} custom-call(bf16[16,1024]{1,0:T(8,128)(2,1)} %queries_hbm.1, s32[1,16]{1,0:T(1,128)} %bitcast.1, bf16[1,4096,128]{2,1,0:T(8,128)(2,1)} %keys.1, bf16[1,4096,128]{2,1,0:T(8,128)(2,1)} %values.1), custom_call_target="tpu_custom_call" | custom-call | flops 2147483648 | bytes 2097152 | tf_op jit(solution)/shard_map/pallas_call | solution.py:272
  37.1 1.4 %copy.6 = bf16[16,1024]{1,0:T(8,128)(2,1)} copy(bf16[16,1024]{1,0:T(8,128)(2,1)} %shard_map.46) | data formatting | bytes 65536

commit v6 on v5

--- a/solution.py
+++ b/solution.py
@@ -198,13 +198,14 @@
             )
 
         def send_part(step):
-            to = pre_at[step]
+            to = lax.rem(pre + step, n_pre)
+            number = to * (n_ctx * n_kvh) + kvh + chunk * n_kvh
             for src, dst, send_sem, recv_sem in (
                 (part, part_in, part_send, part_recv), (stat, stat_in, stat_send, stat_recv)
             ):
                 pltpu.make_async_remote_copy(
                     src_ref=src.at[chunk, to], dst_ref=dst.at[ctx, pre], send_sem=send_sem, recv_sem=recv_sem,
-                    device_id=device(step, chunk), device_id_type=pl.DeviceIdType.LOGICAL,
+                    device_id=number, device_id_type=pl.DeviceIdType.LOGICAL,
                 ).start()
 
         @pl.when(chunk == ctx)
@@ -216,8 +217,7 @@
         def _():
             send_part(0)
 
-        for step in range(1, n_pre):
-            send_part(step)
+        lax.fori_loop(1, n_pre, lambda step, carry: (send_part(step), carry)[1], 0)
         return carry
 
     lax.fori_loop(0, n_ctx, chunk_step, 0)

time: 38.7 us -> 38.8 us (level)
  no operation moved by 1% of the time
where the time goes in v6:
time: 38.8 us; the launch traced here: 38.7 us
  Pallas kernels  37.3 us (96%)
  local copies, waits for them, and re-layouts  1.38 us (4%)
    pallas_call x1, Pallas kernels, body(): pl.pallas_call(functools.partial(kernel, n_pre, n_ctx, block_len), out_sh...  37.3 us
    unnamed x1, local copies, waits for them, and re-layouts  1.38 us

profile of v6, /device:TPU:130, one launch (start us, length us, event | category | flops | bytes accessed | tf_op | source)
XLA Modules:
  0.0 38.7 jit_solution(13948044929435408305)
XLA Ops:
  0.0 37.3 %shard_map.46 = bf16[16,1024]{1,0:T(8,128)(2,1)} custom-call(bf16[16,1024]{1,0:T(8,128)(2,1)} %queries_hbm.1, s32[1,16]{1,0:T(1,128)} %bitcast.1, bf16[1,4096,128]{2,1,0:T(8,128)(2,1)} %keys.1, bf16[1,4096,128]{2,1,0:T(8,128)(2,1)} %values.1), custom_call_target="tpu_custom_call" | custom-call | flops 2147483648 | bytes 2097152 | tf_op jit(solution)/shard_map/pallas_call | solution.py:272
  37.3 1.4 %copy.6 = bf16[16,1024]{1,0:T(8,128)(2,1)} copy(bf16[16,1024]{1,0:T(8,128)(2,1)} %shard_map.46) | data formatting | bytes 65536

commit v7 on v5

--- a/solution.py
+++ b/solution.py
@@ -14,6 +14,7 @@
 VMEM_LIMIT = 63 * 1024 * 1024
 LANES = 128
 PIECE = 512
+WIDE = 1024
 MSG = SEND_CAP * GROUP
 
 
@@ -179,8 +180,8 @@
 
         def weight_step(j, carry):
             added = None
-            for piece in range(block_len // PIECE):
-                span = pl.ds(pl.multiple_of(j * block_len + piece * PIECE, PIECE), PIECE)
+            for piece in range(block_len // WIDE):
+                span = pl.ds(pl.multiple_of(j * block_len + piece * WIDE, WIDE), WIDE)
                 p = jnp.exp2(scores[:, span] * log_scale - top).astype(jnp.bfloat16)
                 more = jnp.dot(p, v_ones[span, :], preferred_element_type=jnp.float32)
                 added = more if added is None else added + more

time: 38.7 us -> 38.7 us (level)
  no operation moved by 1% of the time
where the time goes in v7:
time: 38.7 us; the launch traced here: 38.5 us
  Pallas kernels  37.1 us (96%)
  local copies, waits for them, and re-layouts  1.38 us (4%)
    pallas_call x1, Pallas kernels, body(): pl.pallas_call(functools.partial(kernel, n_pre, n_ctx, block_len), out_sh...  37.1 us
    unnamed x1, local copies, waits for them, and re-layouts  1.38 us

profile of v7, /device:TPU:130, one launch (start us, length us, event | category | flops | bytes accessed | tf_op | source)
XLA Modules:
  0.0 38.5 jit_solution(8250196322858840155)
XLA Ops:
  0.0 37.1 %shard_map.46 = bf16[16,1024]{1,0:T(8,128)(2,1)} custom-call(bf16[16,1024]{1,0:T(8,128)(2,1)} %queries_hbm.1, s32[1,16]{1,0:T(1,128)} %bitcast.1, bf16[1,4096,128]{2,1,0:T(8,128)(2,1)} %keys.1, bf16[1,4096,128]{2,1,0:T(8,128)(2,1)} %values.1), custom_call_target="tpu_custom_call" | custom-call | flops 2147483648 | bytes 2097152 | tf_op jit(solution)/shard_map/pallas_call | solution.py:273
  37.1 1.4 %copy.6 = bf16[16,1024]{1,0:T(8,128)(2,1)} copy(bf16[16,1024]{1,0:T(8,128)(2,1)} %shard_map.46) | data formatting | bytes 65536
